TPU v7x, 32 devices: a whole 2x2x4 slice. The times are simulated.
32 devices in a mesh: band: 16 (over z, x, core), fft: 2 (over y).
Axes of the slice: x: 2, y: 2, z: 4, core: 2. Of those that a mesh axis runs over, the one named last changes fastest.
Arguments:
- orbitals: float32 [32, 64, 4096], P('band', 'fft'), may hold values from -5 to 5
Outputs:
- exchange: float32 [32, 64, 4096], P('band', 'fft')
All inputs are finite; a program needn't handle non-finite values.
Results may differ from a plain program's by a relative error of at most 0.00018.
Values sent between devices are 32-bit elements; how exact they have to be, the bound alone decides.
A program may use at most 64 MiB of HBM per device.

v0:
```python
import functools
import math

import jax
import jax.numpy as jnp
import numpy as np
from jax import lax
from jax.experimental import pallas as pl
from jax.experimental.pallas import tpu as pltpu
from jax.sharding import PartitionSpec as P

GRID = 64
ROUNDS = 2
EXX_FRACTION = 0.25
SCREEN = 0.05
MESH = pl.DeviceIdType.MESH
MIB = 1024 * 1024


def real_modes(length):
    n = np.arange(length)
    rows = [np.cos(2 * np.pi * q * n / length) for q in range(length // 2 + 1)]
    rows += [np.sin(2 * np.pi * q * n / length) for q in range(1, length // 2)]
    matrix = np.array(rows)
    return matrix / np.sqrt((matrix**2).sum(1, keepdims=True))


def split(matrix):
    high = matrix.astype(jnp.bfloat16)
    return high, (matrix - high.astype(np.float64)).astype(jnp.bfloat16)


def matrices():
    modes = real_modes(GRID)
    z_forward = np.kron(np.array([[1.0, 1.0], [1.0, -1.0]]) / np.sqrt(2.0), modes.T)
    out = []
    for matrix in (z_forward, z_forward.T):
        high, low = split(matrix)
        out += [np.concatenate([high, high], 0), np.concatenate([low, np.zeros_like(low)], 0)]
    for matrix in (modes, modes.T):
        high, low = split(matrix)
        out.append(
            np.concatenate(
                [np.concatenate([high, high], 1), np.concatenate([low, np.zeros_like(low)], 1)], 0
            )
        )
    return np.concatenate(out, 0)


def unpack(ref):
    sides = [ref[i * 256 : (i + 1) * 256, :] for i in range(4)]
    across = [ref[1024 + i * 128 : 1152 + i * 128, :] for i in range(2)]
    return [jnp.concatenate(sides[:2], 1), jnp.concatenate(sides[2:], 1)] + across


def mode_numbers():
    half = GRID // 2
    return np.concatenate([np.arange(half + 1), np.arange(1, half)])


def filter_table():
    k = jnp.asarray(mode_numbers(), jnp.float32)
    quarter = GRID // 4
    q = np.concatenate([np.arange(quarter + 1), np.arange(1, quarter)])
    weight = np.where((q == 0) | (q == quarter), 1.0, 2.0) / (GRID // 2)
    ky = jnp.asarray(np.stack([q, GRID // 2 - q], 1), jnp.float32)
    unit = 2.0 * math.pi / GRID
    squares = (
        (k * unit)[:, None, None, None] ** 2
        + (ky * unit)[None, :, :, None] ** 2
        + (k * unit)[None, None, None, :] ** 2
    )
    guarded = jnp.where(squares > 0, squares, 1.0)
    table = jnp.where(
        squares > 0, (1.0 - jnp.exp(-guarded / (4.0 * SCREEN * SCREEN))) / guarded, 0.0
    )
    table = table * jnp.asarray(weight, jnp.float32)[None, :, None, None]
    return table.reshape(GRID, GRID * GRID)


def rotate(c, s, cos, sin):
    return cos * c - sin * s, sin * c + cos * s


def forward(x):
    n = len(x)
    if n == 2:
        return [x[0] + x[1], x[0] - x[1]], {}
    ce, se = forward(x[0::2])
    co, so = forward(x[1::2])
    half, quarter = n // 2, n // 4
    c, s = [None] * (half + 1), {}
    c[0], c[half] = ce[0] + co[0], ce[0] - co[0]
    c[quarter], s[quarter] = ce[quarter], co[quarter]
    for q in range(1, quarter):
        if 8 * q == n:
            r = math.sqrt(0.5)
            a, b = (co[q] - so[q]) * r, (co[q] + so[q]) * r
        else:
            a, b = rotate(co[q], so[q], math.cos(2 * math.pi * q / n), math.sin(2 * math.pi * q / n))
        c[q], c[half - q] = ce[q] + a, ce[q] - a
        s[q], s[half - q] = b + se[q], b - se[q]
    return c, s


def backward(c, s):
    n = 2 * (len(c) - 1)
    if n == 2:
        return [c[0] + c[1], c[0] - c[1]]
    half, quarter = n // 2, n // 4
    ce, co, se, so = [None] * (quarter + 1), [None] * (quarter + 1), {}, {}
    ce[0], co[0] = c[0] + c[half], c[0] - c[half]
    ce[quarter], co[quarter] = c[quarter], s[quarter]
    for q in range(1, quarter):
        ce[q], a = c[q] + c[half - q], c[q] - c[half - q]
        b, se[q] = s[q] + s[half - q], s[q] - s[half - q]
        if 8 * q == n:
            r = math.sqrt(0.5)
            co[q], so[q] = (a + b) * r, (b - a) * r
        else:
            co[q], so[q] = rotate(a, b, math.cos(2 * math.pi * q / n), -math.sin(2 * math.pi * q / n))
    out = [None] * n
    out[0::2], out[1::2] = backward(ce, se), backward(co, so)
    return out


def twiddles(shape, q):
    odd = lax.broadcasted_iota(jnp.int32, shape, 1) >= shape[1] // 2
    angle = 2 * math.pi * q / GRID
    return jnp.where(odd, math.cos(angle), 1.0), jnp.where(odd, math.sin(angle), 0.0)


def halves(value):
    high = value.astype(jnp.bfloat16)
    return high, (value - high.astype(jnp.float32)).astype(jnp.bfloat16)


def along_z(tiles, double):
    high, rest = halves(jnp.concatenate(tiles, 0))
    out = jnp.dot(jnp.concatenate([high, rest], 1), double, preferred_element_type=jnp.float32)
    out = out[:, :LANES] + out[:, LANES:]
    step = tiles[0].shape[0]
    return [out[i * step : (i + 1) * step] for i in range(len(tiles))]


def along_x(value, double):
    length = value.shape[0]
    out = jnp.dot(double, jnp.concatenate(halves(value), 0), preferred_element_type=jnp.float32)
    return out[:length] + out[length:]


LANES = 128
PART = 2048
TABLE_PART = 512


def into_modes(densities):
    count = len(densities)
    quarter = count // 2
    c, s = forward(densities)
    for q in range(1, quarter):
        cos, sin = twiddles(densities[0].shape, q)
        c[q], s[q] = rotate(c[q], s[q], cos, sin)
    return c + [s[q] for q in range(1, quarter)]


def out_of_modes(values):
    quarter = len(values) // 2
    c, s = values[: quarter + 1], dict(enumerate(values[quarter + 1 :], 1))
    for q in range(1, quarter):
        cos, sin = twiddles(values[0].shape, q)
        c[q], s[q] = rotate(c[q], s[q], cos, -sin)
    return backward(c, s)


def filtered(tiles, table, z_forward, z_backward, x_forward, x_backward):
    value = along_x(jnp.concatenate(along_z(tiles, z_forward), 1), x_forward)
    value = along_x(value * table, x_backward)
    return along_z([value[:, i : i + LANES] for i in range(0, value.shape[1], LANES)], z_backward)


def columns(i):
    return slice(i * LANES, (i + 1) * LANES)


def exchange_kernel(orbital_ref, source_ref, filter_ref, *rest):
    constants, out_ref, work = rest
    length, cells = work.shape
    count = cells // LANES

    @pl.loop(0, length // 8)
    def _(block):
        rows = pl.ds(pl.multiple_of(block * 8, 8), 8)
        values = [
            orbital_ref[rows, columns(i)] * source_ref[0, rows, columns(i)] for i in range(count)
        ]
        for i, value in enumerate(into_modes(values)):
            work[rows, columns(i)] = value

    @pl.loop(0, cells // PART)
    def _(part):
        lanes = [pl.ds(pl.multiple_of(part * PART + i, LANES), LANES) for i in range(0, PART, LANES)]
        table = filter_ref[:, pl.ds(pl.multiple_of(part * PART, PART), PART)]
        tiles = filtered([work[:, lane] for lane in lanes], table, *unpack(constants))
        for lane, tile in zip(lanes, tiles):
            work[:, lane] = tile

    first = pl.program_id(0) == 0

    @pl.loop(0, length // 8)
    def _(block):
        rows = pl.ds(pl.multiple_of(block * 8, 8), 8)
        values = out_of_modes([work[rows, columns(i)] for i in range(count)])
        for i, value in enumerate(values):
            term = value * source_ref[0, rows, columns(i)] * -EXX_FRACTION
            out_ref[rows, columns(i)] = jnp.where(first, 0.0, out_ref[rows, columns(i)]) + term


def apply_exchange(orbital, sources):
    count, length, cells = sources.shape
    constants = jnp.asarray(matrices())
    whole = lambda shape: pl.BlockSpec(shape, lambda j: (0, 0))
    return pl.pallas_call(
        exchange_kernel,
        grid=(count,),
        out_shape=jax.ShapeDtypeStruct((length, cells), jnp.float32),
        in_specs=[
            whole((length, cells)),
            pl.BlockSpec((1, length, cells), lambda j: (j, 0, 0)),
            whole((length, cells)),
            whole(constants.shape),
        ],
        out_specs=whole((length, cells)),
        scratch_shapes=[pltpu.VMEM((length, cells), jnp.float32)],
        compiler_params=pltpu.CompilerParams(vmem_limit_bytes=32 * MIB),
        name="exchange",
    )(orbital, sources, filter_table(), constants)


GROUP = 8
COLUMNS = 4
LAG = 2
START = 8
TABLE_PART = 512


def filter_part(part, length):
    shape = (length, TABLE_PART)
    half, quarter = length // 2, length // 4
    lane = lax.broadcasted_iota(jnp.int32, shape, 1) + part * TABLE_PART

    def mode(index):
        return jnp.where(index > half, index - half, index)

    row = lane >> 7
    q = jnp.where(row > quarter, row - quarter, row)
    ky = jnp.where((lane & half * 2) == 0, q, half - q)
    edge = jnp.logical_or(q == 0, q == quarter)
    squares = jnp.zeros(shape, jnp.float32)
    for k in (mode(lax.broadcasted_iota(jnp.int32, shape, 0)), ky, mode(lane & (length - 1))):
        squares = squares + (k.astype(jnp.float32) * (2.0 * math.pi / length)) ** 2
    guarded = jnp.where(squares > 0, squares, 1.0)
    table = (1.0 - jnp.exp(-guarded / (4.0 * SCREEN * SCREEN))) / guarded
    return jnp.where(squares > 0, table, 0.0) * jnp.where(edge, 1.0 / half, 2.0 / half)


def fused_kernel(chips, row, x_ref, matrix_ref, out_ref, *rest):
    (constants, source, orbital, table, work, total, partial, copy_sem, swap_send, swap_recv, beside_send,
     beside_recv, local_sem, scatter_send, up_send, y_send, x_send, own_recv, y_recv, x_recv, d_recv,
     part_send, part_recv, back_send, back_recv, done_send, done_recv) = rest
    band, half = lax.axis_index("band"), lax.axis_index("fft")
    chip, core = band // 2, band % 2
    side, layer = chip % row, chip // row
    owned, planes, cells = x_ref.shape
    length = 2 * planes
    other = 1 - half
    groups, width = planes // GROUP, cells // COLUMNS
    share = groups // 2
    per_orbital = 2 * groups
    pieces = owned * per_orbital
    root, has_up, has_down = chip == 0, chip + row < chips, layer > 0
    across_band, beside_band = band + 2 - 4 * side, band + 1 - 2 * core
    to_y = {"band": band, "fft": other}
    to_core = {"band": beside_band, "fft": half}
    to_cross = {"band": beside_band, "fft": other}
    to_x = {"band": across_band, "fft": half}
    to_diagonal = {"band": across_band, "fft": other}
    to_up = {"band": band + 2 * row, "fft": half}
    to_down = {"band": band - 2 * row, "fft": half}
    own = 2 * side + half
    over_y, over_x, over_both = own + 1 - 2 * half, own + 2 - 4 * side, 3 - own

    barrier = pltpu.get_barrier_semaphore()

    def greet(target):
        pl.semaphore_signal(barrier, inc=1, device_id=target, device_id_type=MESH)

    greet(to_y)
    greet(to_core)
    greet(to_cross)
    greet(to_x)

    @pl.when(has_up)
    def _():
        greet(to_up)

    @pl.when(has_down)
    def _():
        greet(to_down)

    @pl.when(layer == 0)
    def _():
        greet(to_diagonal)

    pl.semaphore_wait(barrier, 5 + has_up.astype(jnp.int32))

    def remote(src, dst, send, recv, target):
        return pltpu.make_async_remote_copy(
            src_ref=src, dst_ref=dst, send_sem=send, recv_sem=recv, device_id=target, device_id_type=MESH
        )

    def send(block, send_sem, recv_sem, target):
        remote(block, block, send_sem, recv_sem, target).start()

    def arrived(block, recv):
        remote(block, block, swap_send, recv, to_y).wait_recv()

    def sent(block, send_sem):
        remote(block, block, send_sem, swap_recv, to_y).wait_send()

    def group_rows(group):
        return pl.ds(pl.multiple_of(group * GROUP, GROUP), GROUP)

    def place(q, column):
        rows = group_rows((q % per_orbital) // 2)
        return q // per_orbital, q % 2, rows, pl.ds(pl.multiple_of(column * width, width), width)

    def piece(q, column):
        return source.at[place(q, column)]

    def outer(q, column):
        o, _, rows, lanes = place(q, column)
        return x_ref.at[o, rows, lanes]

    def local(q):
        return pltpu.make_async_copy(outer(q, own), piece(q, own), local_sem.at[q])

    swap = remote(x_ref.at[other], orbital.at[core, half], swap_send, swap_recv, to_y)
    swap.start()

    @pl.when(root)
    def _():
        @pl.loop(0, pieces)
        def _(q):
            @pl.when(q % 2 == half)
            def _():
                for i, (column, target) in enumerate(
                    ((over_x, to_x), (over_both, to_diagonal), (over_y, to_y))
                ):
                    remote(
                        outer(q, column), piece(q, column), scatter_send.at[i], own_recv.at[q], target
                    ).start()
                local(q).start()

    remote(x_ref.at[half], orbital.at[core, half], beside_send.at[0], beside_recv.at[0], to_core).start()
    keep = pltpu.make_async_copy(x_ref.at[half], orbital.at[core, half], copy_sem.at[0])
    keep.start()
    fetch = pltpu.make_async_copy(matrix_ref, constants, copy_sem.at[1])
    fetch.start()

    def within(q):
        return jnp.logical_and(q >= 0, q < pieces)

    def event(k):
        @pl.when(k < pieces)
        def _():
            block = piece(k, own)
            at_home = jnp.logical_and(root, k % 2 == half)

            @pl.when(at_home)
            def _():
                local(k).wait()

            @pl.when(jnp.logical_not(at_home))
            def _():
                arrived(block, own_recv.at[k])

            @pl.when(has_up)
            def _():
                send(block, up_send, own_recv.at[k], to_up)

            send(block, y_send, y_recv.at[k], to_y)
            send(block, x_send, x_recv.at[k], to_x)

        q = k - LAG

        @pl.when(within(q))
        def _():
            block = piece(q, over_y)
            arrived(block, y_recv.at[q])
            send(block, x_send, d_recv.at[q], to_x)
            arrived(piece(q, over_x), x_recv.at[q])

        r = k - 2 * LAG

        @pl.when(within(r))
        def _():
            arrived(piece(r, over_both), d_recv.at[r])

        @pl.when(k == START - 1)
        def _():
            arrived(orbital.at[core, other], swap_recv)
            send(orbital.at[core, other], beside_send.at[1], beside_recv.at[1], to_core)

        @pl.when(k == START)
        def _():
            keep.wait()
            arrived(orbital.at[1 - core, half], beside_recv.at[0])
            arrived(orbital.at[1 - core, other], beside_recv.at[1])

        t = k - START

        @pl.when(within(t))
        def _():
            o, h, rows = t // per_orbital, t % 2, group_rows((t % per_orbital) // 2)
            to = group_rows(h * groups + (t % per_orbital) // 2)

            @pl.loop(0, 2)
            def _(which):
                values = [
                    orbital[which, h, rows, columns(i)] * source[o, h, rows, columns(i)]
                    for i in range(count)
                ]
                for i, value in enumerate(into_modes(values)):
                    work[2 * o + which, to, columns(i)] = value

    count = cells // LANES
    ahead = per_orbital + START

    @pl.loop(0, ahead)
    def _(k):
        event(k)

        @pl.when(k < cells // TABLE_PART)
        def _():
            lanes = pl.ds(pl.multiple_of(k * TABLE_PART, TABLE_PART), TABLE_PART)
            table[:, lanes] = filter_part(k, length)

    fetch.wait()

    def slot(index, number):
        @pl.when(index < 2)
        def _():
            event(ahead + index * 4 + number)

    @pl.loop(0, 2 * owned)
    def _(index):
        which, o = index % 2, index // 2

        @pl.loop(0, cells // PART)
        def _(part):
            slot(index, part)
            lanes = [pl.ds(pl.multiple_of(part * PART + i, LANES), LANES) for i in range(0, PART, LANES)]
            whole = table[:, pl.ds(pl.multiple_of(part * PART, PART), PART)]
            tiles = filtered([work[index, :, lane] for lane in lanes], whole, *unpack(constants))
            for lane, tile in zip(lanes, tiles):
                work[index, :, lane] = tile

        @pl.loop(0, per_orbital)
        def _(step):
            @pl.when(step % 4 == 0)
            def _():
                slot(index, 2 + step // 4)

            mine = step // groups
            n = step % groups
            h = jnp.where(n < share, other, half)
            holder = jnp.where(mine == 1, core, 1 - core)
            group = holder * share + n % share
            rows, to = group_rows(group), group_rows(h * groups + group)
            values = out_of_modes([work[index, to, columns(i)] for i in range(count)])
            for i, value in enumerate(values):
                term = value * source[o, h, rows, columns(i)] * -EXX_FRACTION
                earlier = jnp.where(o == 0, 0.0, total[which, h, rows, columns(i)])
                total[which, h, rows, columns(i)] = earlier + term

            block = total.at[which, h, rows]
            last = o == owned - 1

            @pl.when(jnp.logical_and(last, mine == 0))
            def _():
                remote(block, partial.at[which, n], part_send, part_recv.at[which, n], to_core).start()

            @pl.when(jnp.logical_and(last, mine == 1))
            def _():
                arrived(partial.at[which, n], part_recv.at[which, n])
                for i in range(count):
                    total[which, h, rows, columns(i)] += partial[which, n, :, columns(i)]
                goal = out_ref.at[half, rows]

                @pl.when(n < share)
                def _():
                    remote(
                        block, goal, back_send, back_recv.at[core], {"band": 2 * chip + which, "fft": other}
                    ).start()

                @pl.when(jnp.logical_and(n >= share, which == core))
                def _():
                    pltpu.make_async_copy(block, goal, copy_sem.at[2]).start()

                @pl.when(jnp.logical_and(n >= share, which != core))
                def _():
                    remote(block, goal, done_send, done_recv, to_core).start()

    @pl.when(has_up)
    def _():
        sent(orbital.at[0, 0], up_send)

    @pl.when(root)
    def _():
        for i in range(3):
            sent(orbital.at[0, 0, : planes // 2], scatter_send.at[i])

    sent(orbital.at[0, 0], y_send)
    sent(orbital.at[0], x_send)
    sent(orbital.at[0, 0], beside_send.at[0])
    sent(orbital.at[0, 0], beside_send.at[1])
    swap.wait_send()
    sent(total.at[0], part_send)
    sent(total.at[0, 0], back_send)
    first, second = out_ref.at[other, : planes // 2], out_ref.at[other, planes // 2 :]
    sent(total.at[0, 0, : planes // 2], done_send)
    arrived(first, done_recv)
    pltpu.make_async_copy(total.at[0, 0, : planes // 2], first, copy_sem.at[2]).wait()
    arrived(first, back_recv.at[0])
    arrived(second, back_recv.at[1])


def two_halves(bands, row, orbitals):
    owned, planes, cells = orbitals.shape
    groups = planes // GROUP
    count = owned * 2 * groups
    dma = pltpu.SemaphoreType.DMA
    constants = jnp.asarray(matrices())
    grid = lambda *lead: pltpu.VMEM((*lead, planes, cells), jnp.float32)
    return pl.pallas_call(
        functools.partial(fused_kernel, bands // 2, row),
        out_shape=jax.ShapeDtypeStruct(orbitals.shape, jnp.float32),
        in_specs=[pl.BlockSpec(memory_space=pl.ANY)] * 2,
        out_specs=pl.BlockSpec(memory_space=pl.ANY),
        scratch_shapes=[
            pltpu.VMEM(constants.shape, jnp.bfloat16),
            grid(owned, 2),
            grid(2, 2),
            pltpu.VMEM((2 * planes, cells), jnp.float32),
            pltpu.VMEM((2 * owned, 2 * planes, cells), jnp.float32),
            grid(2, 2),
            pltpu.VMEM((2, groups, GROUP, cells), jnp.float32),
        ]
        + [dma((3,)), dma, dma, dma((2,)), dma((2,)), dma((count,)), dma((3,))]
        + [dma] * 3
        + [dma((count,))] * 4
        + [dma, dma((2, groups)), dma, dma((2,)), dma, dma],
        compiler_params=pltpu.CompilerParams(
            collective_id=0, has_side_effects=True, vmem_limit_bytes=60 * MIB
        ),
        name="exchange",
    )(orbitals, constants)


def many_parts(parts, orbitals):
    owned = orbitals.shape[0]
    place, band = lax.axis_index("fft"), lax.axis_index("band")
    fields = lax.all_gather(orbitals, "fft", axis=1, tiled=True)
    held = jnp.concatenate([jnp.where(band == r, fields, 0.0) for r in range(ROUNDS)], 0)
    sources = lax.psum(held, "band")
    groups = max(parts // owned, 1)
    share = sources.shape[0] // groups
    mine = lax.dynamic_slice_in_dim(sources, (place // owned) * share, share, 0)
    which = place % owned
    result = apply_exchange(lax.dynamic_index_in_dim(fields, which, 0, False), mine)
    placed = jnp.where(jnp.arange(owned)[:, None, None] == which, result[None], 0.0)
    return lax.psum_scatter(placed, "fft", scatter_dimension=1, tiled=True)


def solution(mesh):
    parts = mesh.shape["fft"]
    if parts == 2:
        body = functools.partial(two_halves, mesh.shape["band"], 2)
    else:
        body = functools.partial(many_parts, parts)
    return jax.shard_map(
        body, mesh=mesh, in_specs=(P("band", "fft", None),), out_specs=P("band", "fft", None), check_vma=False
    )
```

profile of v0, /device:TPU:25, one launch (start us, length us, event | category | flops | bytes accessed | tf_op | source)
XLA Modules:
  0.0 76.9 jit_solution(9786611964545950242)
XLA Ops:
  0.0 74.6 %exchange.1 = f32[2,32,4096]{2,1,0:T(8,128)} custom-call(f32[2,32,4096]{2,1,0:T(8,128)} %x_ref.1, bf16[1280,128]{1,0:T(8,128)(2,1)} %constant.2.clone.matrix_ref), custom_call_target="tpu_custom_call" | custom-call | tf_op jit(solution)/shard_map/exchange/pallas_call | solution.py:546
  74.6 2.3 %copy.4 = f32[2,32,4096]{2,1,0:T(8,128)} copy(f32[2,32,4096]{2,1,0:T(8,128)} %exchange.1) | data formatting | bytes 2097152
where the time goes:
time: 77.1 us; the launch traced here: 76.9 us
  Pallas kernels  74.6 us (97%)
  local copies, waits for them, and re-layouts  2.27 us (3%)
    pallas_call x1, Pallas kernels, two_halves(): pl.pallas_call(functools.partial(fused_kernel, bands // 2, row), out_shap...  74.6 us
    unnamed x1, local copies, waits for them, and re-layouts  2.27 us

commit v1 on v0

--- a/solution.py
+++ b/solution.py
@@ -240,7 +240,6 @@
 GROUP = 8
 COLUMNS = 4
 LAG = 2
-START = 8
 TABLE_PART = 512
 
 
@@ -266,7 +265,7 @@
 
 def fused_kernel(chips, row, x_ref, matrix_ref, out_ref, *rest):
     (constants, source, orbital, table, work, total, partial, copy_sem, swap_send, swap_recv, beside_send,
-     beside_recv, local_sem, scatter_send, up_send, y_send, x_send, own_recv, y_recv, x_recv, d_recv,
+     beside_recv, local_sem, scatter_send, up_send, far_send, y_send, x_send, own_recv, y_recv, x_recv, d_recv,
      part_send, part_recv, back_send, back_recv, done_send, done_recv) = rest
     band, half = lax.axis_index("band"), lax.axis_index("fft")
     chip, core = band // 2, band % 2
@@ -278,7 +277,7 @@
     share = groups // 2
     per_orbital = 2 * groups
     pieces = owned * per_orbital
-    root, has_up, has_down = chip == 0, chip + row < chips, layer > 0
+    root, has_up, bottom = chip == 0, layer % 2 == 0, layer == 0
     across_band, beside_band = band + 2 - 4 * side, band + 1 - 2 * core
     to_y = {"band": band, "fft": other}
     to_core = {"band": beside_band, "fft": half}
@@ -286,7 +285,8 @@
     to_x = {"band": across_band, "fft": half}
     to_diagonal = {"band": across_band, "fft": other}
     to_up = {"band": band + 2 * row, "fft": half}
-    to_down = {"band": band - 2 * row, "fft": half}
+    to_far = {"band": band + 4 * row, "fft": half}
+    to_down = {"band": band - 2 * row * jnp.where(layer == 2, 2, 1), "fft": half}
     own = 2 * side + half
     over_y, over_x, over_both = own + 1 - 2 * half, own + 2 - 4 * side, 3 - own
 
@@ -304,15 +304,16 @@
     def _():
         greet(to_up)
 
-    @pl.when(has_down)
+    @pl.when(jnp.logical_not(bottom))
     def _():
         greet(to_down)
 
-    @pl.when(layer == 0)
+    @pl.when(bottom)
     def _():
         greet(to_diagonal)
-
-    pl.semaphore_wait(barrier, 5 + has_up.astype(jnp.int32))
+        greet(to_far)
+
+    pl.semaphore_wait(barrier, 5 + has_up.astype(jnp.int32) + bottom.astype(jnp.int32))
 
     def remote(src, dst, send, recv, target):
         return pltpu.make_async_remote_copy(
@@ -385,6 +386,10 @@
             def _():
                 arrived(block, own_recv.at[k])
 
+            @pl.when(bottom)
+            def _():
+                send(block, far_send, own_recv.at[k], to_far)
+
             @pl.when(has_up)
             def _():
                 send(block, up_send, own_recv.at[k], to_up)
@@ -407,35 +412,8 @@
         def _():
             arrived(piece(r, over_both), d_recv.at[r])
 
-        @pl.when(k == START - 1)
-        def _():
-            arrived(orbital.at[core, other], swap_recv)
-            send(orbital.at[core, other], beside_send.at[1], beside_recv.at[1], to_core)
-
-        @pl.when(k == START)
-        def _():
-            keep.wait()
-            arrived(orbital.at[1 - core, half], beside_recv.at[0])
-            arrived(orbital.at[1 - core, other], beside_recv.at[1])
-
-        t = k - START
-
-        @pl.when(within(t))
-        def _():
-            o, h, rows = t // per_orbital, t % 2, group_rows((t % per_orbital) // 2)
-            to = group_rows(h * groups + (t % per_orbital) // 2)
-
-            @pl.loop(0, 2)
-            def _(which):
-                values = [
-                    orbital[which, h, rows, columns(i)] * source[o, h, rows, columns(i)]
-                    for i in range(count)
-                ]
-                for i, value in enumerate(into_modes(values)):
-                    work[2 * o + which, to, columns(i)] = value
-
     count = cells // LANES
-    ahead = per_orbital + START
+    ahead = per_orbital + 2 * LAG
 
     @pl.loop(0, ahead)
     def _(k):
@@ -446,20 +424,47 @@
             lanes = pl.ds(pl.multiple_of(k * TABLE_PART, TABLE_PART), TABLE_PART)
             table[:, lanes] = filter_part(k, length)
 
+        @pl.when(k == ahead - 2)
+        def _():
+            arrived(orbital.at[core, other], swap_recv)
+            send(orbital.at[core, other], beside_send.at[1], beside_recv.at[1], to_core)
+
+    keep.wait()
+    arrived(orbital.at[1 - core, half], beside_recv.at[0])
+    arrived(orbital.at[1 - core, other], beside_recv.at[1])
     fetch.wait()
 
     def slot(index, number):
-        @pl.when(index < 2)
+        @pl.when(index == 0)
         def _():
-            event(ahead + index * 4 + number)
+            event(ahead + number)
 
     @pl.loop(0, 2 * owned)
     def _(index):
         which, o = index % 2, index // 2
 
+        @pl.when(which == 0)
+        def _():
+            @pl.loop(0, per_orbital)
+            def _(block):
+                @pl.when(block % 2 == 0)
+                def _():
+                    slot(index, block // 2)
+
+                h, rows, to = block // groups, group_rows(block % groups), group_rows(block)
+
+                @pl.loop(0, 2)
+                def _(field):
+                    values = [
+                        orbital[field, h, rows, columns(i)] * source[o, h, rows, columns(i)]
+                        for i in range(count)
+                    ]
+                    for i, value in enumerate(into_modes(values)):
+                        work[2 * o + field, to, columns(i)] = value
+
         @pl.loop(0, cells // PART)
         def _(part):
-            slot(index, part)
+            slot(index, 4 + part)
             lanes = [pl.ds(pl.multiple_of(part * PART + i, LANES), LANES) for i in range(0, PART, LANES)]
             whole = table[:, pl.ds(pl.multiple_of(part * PART, PART), PART)]
             tiles = filtered([work[index, :, lane] for lane in lanes], whole, *unpack(constants))
@@ -470,7 +475,7 @@
         def _(step):
             @pl.when(step % 4 == 0)
             def _():
-                slot(index, 2 + step // 4)
+                slot(index, 6 + step // 4)
 
             mine = step // groups
             n = step % groups
@@ -515,6 +520,10 @@
     @pl.when(has_up)
     def _():
         sent(orbital.at[0, 0], up_send)
+
+    @pl.when(bottom)
+    def _():
+        sent(orbital.at[0, 0], far_send)
 
     @pl.when(root)
     def _():
@@ -558,7 +567,7 @@
             pltpu.VMEM((2, groups, GROUP, cells), jnp.float32),
         ]
         + [dma((3,)), dma, dma, dma((2,)), dma((2,)), dma((count,)), dma((3,))]
-        + [dma] * 3
+        + [dma] * 4
         + [dma((count,))] * 4
         + [dma, dma((2, groups)), dma, dma((2,)), dma, dma],
         compiler_params=pltpu.CompilerParams(
@@ -585,7 +594,7 @@
 
 def solution(mesh):
     parts = mesh.shape["fft"]
-    if parts == 2:
+    if parts == 2 and mesh.shape["band"] == 16:
         body = functools.partial(two_halves, mesh.shape["band"], 2)
     else:
         body = functools.partial(many_parts, parts)

time: 77.1 us -> 75.4 us (0.978)
  Pallas kernels: 74.6 us -> 72.9 us
    pallas_call x1, Pallas kernels: 74.6 us -> 72.9 us  [two_halves(): pl.pallas_call(functools.partial(fused_kernel, bands // 2, row), out_shap...]
where the time goes in v1:
time: 75.4 us; the launch traced here: 75.2 us
  Pallas kernels  72.9 us (97%)
  local copies, waits for them, and re-layouts  2.27 us (3%)
    pallas_call x1, Pallas kernels, two_halves(): pl.pallas_call(functools.partial(fused_kernel, bands // 2, row), out_shap...  72.9 us
    unnamed x1, local copies, waits for them, and re-layouts  2.27 us

profile of v1, /device:TPU:25, one launch (start us, length us, event | category | flops | bytes accessed | tf_op | source)
XLA Modules:
  0.0 75.2 jit_solution(3394464704407016445)
XLA Ops:
  0.0 72.9 %exchange.1 = f32[2,32,4096]{2,1,0:T(8,128)} custom-call(f32[2,32,4096]{2,1,0:T(8,128)} %x_ref.1, bf16[1280,128]{1,0:T(8,128)(2,1)} %constant.2.clone.matrix_ref), custom_call_target="tpu_custom_call" | custom-call | tf_op jit(solution)/shard_map/exchange/pallas_call | solution.py:555
  72.9 2.3 %copy.4 = f32[2,32,4096]{2,1,0:T(8,128)} copy(f32[2,32,4096]{2,1,0:T(8,128)} %exchange.1) | data formatting | bytes 2097152

commit v2 on v1

--- a/solution.py
+++ b/solution.py
@@ -150,7 +150,7 @@
 
 
 LANES = 128
-PART = 2048
+PART = 512
 TABLE_PART = 512
 
 
@@ -260,7 +260,8 @@
         squares = squares + (k.astype(jnp.float32) * (2.0 * math.pi / length)) ** 2
     guarded = jnp.where(squares > 0, squares, 1.0)
     table = (1.0 - jnp.exp(-guarded / (4.0 * SCREEN * SCREEN))) / guarded
-    return jnp.where(squares > 0, table, 0.0) * jnp.where(edge, 1.0 / half, 2.0 / half)
+    scale = -EXX_FRACTION / half
+    return jnp.where(squares > 0, table, 0.0) * jnp.where(edge, scale, 2.0 * scale)
 
 
 def fused_kernel(chips, row, x_ref, matrix_ref, out_ref, *rest):
@@ -462,11 +463,11 @@
                     for i, value in enumerate(into_modes(values)):
                         work[2 * o + field, to, columns(i)] = value
 
-        @pl.loop(0, cells // PART)
-        def _(part):
-            slot(index, 4 + part)
-            lanes = [pl.ds(pl.multiple_of(part * PART + i, LANES), LANES) for i in range(0, PART, LANES)]
-            whole = table[:, pl.ds(pl.multiple_of(part * PART, PART), PART)]
+        for part in range(cells // PART):
+            if part % 4 == 0:
+                slot(index, 4 + part // 4)
+            lanes = [slice(part * PART + i, part * PART + i + LANES) for i in range(0, PART, LANES)]
+            whole = table[:, part * PART : (part + 1) * PART]
             tiles = filtered([work[index, :, lane] for lane in lanes], whole, *unpack(constants))
             for lane, tile in zip(lanes, tiles):
                 work[index, :, lane] = tile
@@ -485,7 +486,7 @@
             rows, to = group_rows(group), group_rows(h * groups + group)
             values = out_of_modes([work[index, to, columns(i)] for i in range(count)])
             for i, value in enumerate(values):
-                term = value * source[o, h, rows, columns(i)] * -EXX_FRACTION
+                term = value * source[o, h, rows, columns(i)]
                 earlier = jnp.where(o == 0, 0.0, total[which, h, rows, columns(i)])
                 total[which, h, rows, columns(i)] = earlier + term
 

time: 75.4 us -> 79.9 us (1.060)
  Pallas kernels: 72.9 us -> 77.4 us
    pallas_call x1, Pallas kernels: 72.9 us -> 77.4 us  [two_halves(): pl.pallas_call(functools.partial(fused_kernel, bands // 2, row), out_shap...]
where the time goes in v2:
time: 79.9 us; the launch traced here: 79.7 us
  Pallas kernels  77.4 us (97%)
  local copies, waits for them, and re-layouts  2.27 us (3%)
    pallas_call x1, Pallas kernels, two_halves(): pl.pallas_call(functools.partial(fused_kernel, bands // 2, row), out_shap...  77.4 us
    unnamed x1, local copies, waits for them, and re-layouts  2.27 us

profile of v2, /device:TPU:25, one launch (start us, length us, event | category | flops | bytes accessed | tf_op | source)
XLA Modules:
  0.0 79.7 jit_solution(2890194208278056138)
XLA Ops:
  0.0 77.4 %exchange.1 = f32[2,32,4096]{2,1,0:T(8,128)} custom-call(f32[2,32,4096]{2,1,0:T(8,128)} %x_ref.1, bf16[1280,128]{1,0:T(8,128)(2,1)} %constant.2.clone.matrix_ref), custom_call_target="tpu_custom_call" | custom-call | tf_op jit(solution)/shard_map/exchange/pallas_call | solution.py:556
  77.4 2.3 %copy.4 = f32[2,32,4096]{2,1,0:T(8,128)} copy(f32[2,32,4096]{2,1,0:T(8,128)} %exchange.1) | data formatting | bytes 2097152

commit v3 on v2

--- a/solution.py
+++ b/solution.py
@@ -150,7 +150,7 @@
 
 
 LANES = 128
-PART = 512
+PART = 4096
 TABLE_PART = 512
 
 
@@ -347,8 +347,11 @@
     def local(q):
         return pltpu.make_async_copy(outer(q, own), piece(q, own), local_sem.at[q])
 
-    swap = remote(x_ref.at[other], orbital.at[core, half], swap_send, swap_recv, to_y)
-    swap.start()
+    def swap(k):
+        rows, lanes = group_rows(k // 2), pl.ds(pl.multiple_of(k % 2 * (cells // 2), cells // 2), cells // 2)
+        return remote(
+            x_ref.at[other, rows, lanes], orbital.at[core, half, rows, lanes], swap_send, swap_recv, to_y
+        )
 
     @pl.when(root)
     def _():
@@ -397,6 +400,10 @@
 
             send(block, y_send, y_recv.at[k], to_y)
             send(block, x_send, x_recv.at[k], to_x)
+
+        @pl.when(k < per_orbital)
+        def _():
+            swap(k).start()
 
         q = k - LAG
 
@@ -464,8 +471,8 @@
                         work[2 * o + field, to, columns(i)] = value
 
         for part in range(cells // PART):
-            if part % 4 == 0:
-                slot(index, 4 + part // 4)
+            slot(index, 4)
+            slot(index, 5)
             lanes = [slice(part * PART + i, part * PART + i + LANES) for i in range(0, PART, LANES)]
             whole = table[:, part * PART : (part + 1) * PART]
             tiles = filtered([work[index, :, lane] for lane in lanes], whole, *unpack(constants))
@@ -535,7 +542,7 @@
     sent(orbital.at[0], x_send)
     sent(orbital.at[0, 0], beside_send.at[0])
     sent(orbital.at[0, 0], beside_send.at[1])
-    swap.wait_send()
+    sent(orbital.at[0, 0], swap_send)
     sent(total.at[0], part_send)
     sent(total.at[0, 0], back_send)
     first, second = out_ref.at[other, : planes // 2], out_ref.at[other, planes // 2 :]

time: 79.9 us -> 69.9 us (0.87)
  Pallas kernels: 77.4 us -> 67.5 us
    pallas_call x1, Pallas kernels: 77.4 us -> 67.5 us  [two_halves(): pl.pallas_call(functools.partial(fused_kernel, bands // 2, row), out_shap...]
where the time goes in v3:
time: 69.9 us; the launch traced here: 69.7 us
  Pallas kernels  67.5 us (97%)
  local copies, waits for them, and re-layouts  2.27 us (3%)
    pallas_call x1, Pallas kernels, two_halves(): pl.pallas_call(functools.partial(fused_kernel, bands // 2, row), out_shap...  67.5 us
    unnamed x1, local copies, waits for them, and re-layouts  2.27 us

profile of v3, /device:TPU:25, one launch (start us, length us, event | category | flops | bytes accessed | tf_op | source)
XLA Modules:
  0.0 69.7 jit_solution(6833549425406596690)
XLA Ops:
  0.0 67.5 %exchange.1 = f32[2,32,4096]{2,1,0:T(8,128)} custom-call(f32[2,32,4096]{2,1,0:T(8,128)} %x_ref.1, bf16[1280,128]{1,0:T(8,128)(2,1)} %constant.2.clone.matrix_ref), custom_call_target="tpu_custom_call" | custom-call | tf_op jit(solution)/shard_map/exchange/pallas_call | solution.py:563
  67.5 2.3 %copy.4 = f32[2,32,4096]{2,1,0:T(8,128)} copy(f32[2,32,4096]{2,1,0:T(8,128)} %exchange.1) | data formatting | bytes 2097152

commit v4 on v3

--- a/solution.py
+++ b/solution.py
@@ -239,7 +239,7 @@
 
 GROUP = 8
 COLUMNS = 4
-LAG = 2
+LAG = 3
 TABLE_PART = 512
 
 
@@ -260,7 +260,7 @@
         squares = squares + (k.astype(jnp.float32) * (2.0 * math.pi / length)) ** 2
     guarded = jnp.where(squares > 0, squares, 1.0)
     table = (1.0 - jnp.exp(-guarded / (4.0 * SCREEN * SCREEN))) / guarded
-    scale = -EXX_FRACTION / half
+    scale = 1.0 / half
     return jnp.where(squares > 0, table, 0.0) * jnp.where(edge, scale, 2.0 * scale)
 
 
@@ -560,7 +560,7 @@
     dma = pltpu.SemaphoreType.DMA
     constants = jnp.asarray(matrices())
     grid = lambda *lead: pltpu.VMEM((*lead, planes, cells), jnp.float32)
-    return pl.pallas_call(
+    exchange = pl.pallas_call(
         functools.partial(fused_kernel, bands // 2, row),
         out_shape=jax.ShapeDtypeStruct(orbitals.shape, jnp.float32),
         in_specs=[pl.BlockSpec(memory_space=pl.ANY)] * 2,
@@ -583,6 +583,7 @@
         ),
         name="exchange",
     )(orbitals, constants)
+    return -EXX_FRACTION * exchange
 
 
 def many_parts(parts, orbitals):

time: 69.9 us -> 67.6 us (0.967)
  Pallas kernels: 67.5 us -> 64.7 us
  other arithmetic: 0 us -> 2.27 us
  local copies, waits for them, and re-layouts: 2.27 us -> 0 us
    pallas_call x1, Pallas kernels: 67.5 us -> 64.7 us  [two_halves(): pl.pallas_call(functools.partial(fused_kernel, bands // 2, row), out_shap...]
    mul x0 -> x1, other arithmetic: none -> 2.27 us  [two_halves(): return -EXX_FRACTION * exchange]
    unnamed x1 -> x0, local copies, waits for them, and re-layouts: 2.27 us -> none
where the time goes in v4:
time: 67.6 us; the launch traced here: 67 us
  Pallas kernels  64.7 us (96%)
  other arithmetic  2.27 us (3%)
    pallas_call x1, Pallas kernels, two_halves(): pl.pallas_call(functools.partial(fused_kernel, bands // 2, row), out_shap...  64.7 us
    mul x1, other arithmetic, two_halves(): return -EXX_FRACTION * exchange  2.27 us

profile of v4, /device:TPU:25, one launch (start us, length us, event | category | flops | bytes accessed | tf_op | source)
XLA Modules:
  0.0 67.0 jit_solution(15666423892490228654)
XLA Ops:
  0.0 64.7 %exchange.1 = f32[2,32,4096]{2,1,0:T(8,128)} custom-call(f32[2,32,4096]{2,1,0:T(8,128)} %x_ref.1, bf16[1280,128]{1,0:T(8,128)(2,1)} %constant.4.clone.matrix_ref), custom_call_target="tpu_custom_call" | custom-call | tf_op jit(solution)/shard_map/exchange/pallas_call | solution.py:563
  64.8 2.3 %broadcast_multiply_fusion = f32[2,32,4096]{2,1,0:T(8,128)} fusion(f32[2,32,4096]{2,1,0:T(8,128)} %exchange.1), kind=kLoop, calls=%fused_computation | loop fusion | flops 262144 | bytes 2097152 | tf_op jit(solution)/shard_map/mul | solution.py:586

commit v5 on v4

--- a/solution.py
+++ b/solution.py
@@ -240,6 +240,7 @@
 GROUP = 8
 COLUMNS = 4
 LAG = 3
+AHEAD = 4
 TABLE_PART = 512
 
 
@@ -353,19 +354,20 @@
             x_ref.at[other, rows, lanes], orbital.at[core, half, rows, lanes], swap_send, swap_recv, to_y
         )
 
-    @pl.when(root)
-    def _():
-        @pl.loop(0, pieces)
-        def _(q):
-            @pl.when(q % 2 == half)
-            def _():
-                for i, (column, target) in enumerate(
-                    ((over_x, to_x), (over_both, to_diagonal), (over_y, to_y))
-                ):
-                    remote(
-                        outer(q, column), piece(q, column), scatter_send.at[i], own_recv.at[q], target
-                    ).start()
-                local(q).start()
+    def scatter(q):
+        @pl.when(jnp.logical_and(root, jnp.logical_and(q < pieces, q % 2 == half)))
+        def _():
+            for i, (column, target) in enumerate(
+                ((over_x, to_x), (over_both, to_diagonal), (over_y, to_y))
+            ):
+                remote(
+                    outer(q, column), piece(q, column), scatter_send.at[i], own_recv.at[q], target
+                ).start()
+            local(q).start()
+
+    @pl.loop(0, AHEAD)
+    def _(q):
+        scatter(q)
 
     remote(x_ref.at[half], orbital.at[core, half], beside_send.at[0], beside_recv.at[0], to_core).start()
     keep = pltpu.make_async_copy(x_ref.at[half], orbital.at[core, half], copy_sem.at[0])
@@ -400,6 +402,8 @@
 
             send(block, y_send, y_recv.at[k], to_y)
             send(block, x_send, x_recv.at[k], to_x)
+
+        scatter(k + AHEAD)
 
         @pl.when(k < per_orbital)
         def _():

time: 67.6 us -> 67.5 us (level)
  no operation moved by 1% of the time
where the time goes in v5:
time: 67.5 us; the launch traced here: 67.1 us
  Pallas kernels  64.8 us (96%)
  other arithmetic  2.27 us (3%)
    pallas_call x1, Pallas kernels, two_halves(): pl.pallas_call(functools.partial(fused_kernel, bands // 2, row), out_shap...  64.8 us
    mul x1, other arithmetic, two_halves(): return -EXX_FRACTION * exchange  2.27 us

profile of v5, /device:TPU:25, one launch (start us, length us, event | category | flops | bytes accessed | tf_op | source)
XLA Modules:
  0.0 67.1 jit_solution(5494169262301216584)
XLA Ops:
  0.0 64.8 %exchange.1 = f32[2,32,4096]{2,1,0:T(8,128)} custom-call(f32[2,32,4096]{2,1,0:T(8,128)} %x_ref.1, bf16[1280,128]{1,0:T(8,128)(2,1)} %constant.4.clone.matrix_ref), custom_call_target="tpu_custom_call" | custom-call | tf_op jit(solution)/shard_map/exchange/pallas_call | solution.py:567
  64.8 2.3 %broadcast_multiply_fusion = f32[2,32,4096]{2,1,0:T(8,128)} fusion(f32[2,32,4096]{2,1,0:T(8,128)} %exchange.1), kind=kLoop, calls=%fused_computation | loop fusion | flops 262144 | bytes 2097152 | tf_op jit(solution)/shard_map/mul | solution.py:590

commit v6 on v5

--- a/solution.py
+++ b/solution.py
@@ -239,7 +239,7 @@
 
 GROUP = 8
 COLUMNS = 4
-LAG = 3
+LAG = 4
 AHEAD = 4
 TABLE_PART = 512
 

time: 67.5 us -> 66.5 us (0.985)
  Pallas kernels: 64.8 us -> 63.9 us
    pallas_call x1, Pallas kernels: 64.8 us -> 63.9 us  [two_halves(): pl.pallas_call(functools.partial(fused_kernel, bands // 2, row), out_shap...]
where the time goes in v6:
time: 66.5 us; the launch traced here: 66.2 us
  Pallas kernels  63.9 us (96%)
  other arithmetic  2.27 us (3%)
    pallas_call x1, Pallas kernels, two_halves(): pl.pallas_call(functools.partial(fused_kernel, bands // 2, row), out_shap...  63.9 us
    mul x1, other arithmetic, two_halves(): return -EXX_FRACTION * exchange  2.27 us

profile of v6, /device:TPU:25, one launch (start us, length us, event | category | flops | bytes accessed | tf_op | source)
XLA Modules:
  0.0 66.2 jit_solution(5654391631051901775)
XLA Ops:
  0.0 63.9 %exchange.1 = f32[2,32,4096]{2,1,0:T(8,128)} custom-call(f32[2,32,4096]{2,1,0:T(8,128)} %x_ref.1, bf16[1280,128]{1,0:T(8,128)(2,1)} %constant.4.clone.matrix_ref), custom_call_target="tpu_custom_call" | custom-call | tf_op jit(solution)/shard_map/exchange/pallas_call | solution.py:567
  63.9 2.3 %broadcast_multiply_fusion = f32[2,32,4096]{2,1,0:T(8,128)} fusion(f32[2,32,4096]{2,1,0:T(8,128)} %exchange.1), kind=kLoop, calls=%fused_computation | loop fusion | flops 262144 | bytes 2097152 | tf_op jit(solution)/shard_map/mul | solution.py:590
